TPU v7x, 32 devices: a whole 2x2x4 slice. The times are simulated.
32 devices in a mesh: samp: 8 (over z, y), var: 4 (over x, core).
Axes of the slice: x: 2, y: 2, z: 4, core: 2. Of those that a mesh axis runs over, the one named last changes fastest.
Arguments:
- genotypes: int32 [2048, 4096], P('samp', 'var'), may hold values from -1 to 2, as said below
- ancestry: float32 [16, 2048], P(None, 'samp'), may hold values from 0.05 to 4, as said below
- frequency: float32 [16, 4096], P(None, 'var'), may hold values from 0.05 to 0.95
Outputs:
- new_ancestry: float32 [16, 2048], P(None, 'samp')
- new_frequency: float32 [16, 4096], P(None, 'var')
Inputs may be any that keep to these rules, and one draw needn't show every extreme that they name: `genotypes`: A dosage of 0, 1 or 2 alternate alleles, or -1 for a missing genotype. `ancestry`: positive weights.
All inputs are finite; a program needn't handle non-finite values.
Results may differ from a plain program's by a relative error of at most 0.0003.
Values sent between devices are 32-bit elements; how exact they have to be, the bound alone decides.
A program may use at most 64 MiB of HBM per device.

v0:
```python
import jax
import jax.numpy as jnp
from jax import lax
from jax.sharding import PartitionSpec as P

ITERS = 4
HIGH = lax.Precision.HIGHEST


def contract(left, right, left_dim, right_dim):
    return lax.dot_general(
        left,
        right,
        (((left_dim,), (right_dim,)), ((), ())),
        precision=HIGH,
        preferred_element_type=jnp.float32,
    )


def shards(genotypes, ancestry, frequency):
    present = (genotypes >= 0).astype(jnp.float32)
    dosage = jnp.maximum(genotypes, 0).astype(jnp.float32)
    weight_ref = present * dosage
    weight_alt = present * (2.0 - dosage)
    fraction = ancestry / jnp.sum(ancestry, axis=0, keepdims=True)
    for sweep in range(ITERS):
        expected = contract(fraction, frequency, 0, 0)
        ratio_ref = weight_ref / expected
        ratio_alt = weight_alt / (1.0 - expected)
        partial_value = contract(frequency, ratio_ref, 1, 1) + contract(
            1.0 - frequency, ratio_alt, 1, 1
        )
        total = lax.psum(partial_value, "var")
        weighted = fraction * total
        fraction = weighted / jnp.sum(weighted, axis=0, keepdims=True)
        expected = contract(fraction, frequency, 0, 0)
        ratio_ref = weight_ref / expected
        ratio_alt = weight_alt / (1.0 - expected)
        term_ref = contract(fraction, ratio_ref, 1, 0)
        term_alt = contract(fraction, ratio_alt, 1, 0)
        sum_ref, sum_alt = lax.psum((term_ref, term_alt), "samp")
        upper = frequency * sum_ref
        lower = (1.0 - frequency) * sum_alt
        frequency = upper / (upper + lower)
    return (fraction, frequency)


def solution(mesh):
    return jax.shard_map(
        shards,
        mesh=mesh,
        in_specs=(P("samp", "var"), P(None, "samp"), P(None, "var")),
        out_specs=(P(None, "samp"), P(None, "var")),
        check_vma=False,
    )
```

profile of v0, /device:TPU:0, one launch (start us, length us, event | category | flops | bytes accessed | tf_op | source)
XLA Modules:
  0.0 370.3 jit_solution(9430064719370559565)
XLA Ops:
  8.1 1.9 fusion.36
  10.0 1.1 convolution_bitcast_fusion
  11.1 1.1 convolution_add_fusion.3
  12.2 12.7 %psum.84 = f32[16,256]{1,0:T(8,128)S(1)} all-reduce(f32[16,256]{1,0:T(8,128)S(1)} %convolution_add_fusion.3), channel_id=1, replica_groups=mesh['samp'=8,'var'=4] {'var'}, use_global_device_ids=true, to_apply=%region_1.0 | all-reduce | flops 4096 | bytes 32768 | tf_op jit(solution)/shard_map/psum | solution.py:33
  25.9 1.5 fusion.15
  27.5 1.5 fusion.12
  29.0 70.3 %all-reduce.15.cloned.1.call-done = (f32[16,1024]{1,0:T(8,128)}, f32[16,1024]{1,0:T(8,128)}) async-done(((f32[16,1024]{1,0:T(8,128)}, f32[16,1024]{1,0:T(8,128)}), (f32[16,1024]{1,0:T(8,128)}, f32[16,1024]{1,0:T(8,128)})) %all-reduce.15.cloned.1.call-update) | async-done | bytes 131088 | tf_op jit(solution)/shard_map/psum | solution.py:41
  102.3 1.1 convolution_add_fusion.2
  103.4 10.1 %psum.87 = f32[16,256]{1,0:T(8,128)S(1)} all-reduce(f32[16,256]{1,0:T(8,128)S(1)} %convolution_add_fusion.2), channel_id=1, replica_groups=mesh['samp'=8,'var'=4] {'var'}, use_global_device_ids=true, to_apply=%region_5.0 | all-reduce | flops 4096 | bytes 32768 | tf_op jit(solution)/shard_map/psum | solution.py:33
  113.5 1.0 fusion.48
  114.5 1.5 fusion.16
  116.1 1.5 fusion.8
  117.8 69.2 %all-reduce.13.cloned.1.call-done = (f32[16,1024]{1,0:T(8,128)}, f32[16,1024]{1,0:T(8,128)}) async-done(((f32[16,1024]{1,0:T(8,128)}, f32[16,1024]{1,0:T(8,128)}), (f32[16,1024]{1,0:T(8,128)}, f32[16,1024]{1,0:T(8,128)})) %all-reduce.13.cloned.1.call-update) | async-done | bytes 131088 | tf_op jit(solution)/shard_map/psum | solution.py:41
  189.9 1.1 convolution_add_fusion.1
  191.0 10.1 %psum.90 = f32[16,256]{1,0:T(8,128)S(1)} all-reduce(f32[16,256]{1,0:T(8,128)S(1)} %convolution_add_fusion.1), channel_id=1, replica_groups=mesh['samp'=8,'var'=4] {'var'}, use_global_device_ids=true, to_apply=%region_9.0 | all-reduce | flops 4096 | bytes 32768 | tf_op jit(solution)/shard_map/psum | solution.py:33
  202.2 1.5 fusion.17
  203.7 1.5 fusion.4
  205.2 69.4 %all-reduce.11.cloned.1.call-done = (f32[16,1024]{1,0:T(8,128)}, f32[16,1024]{1,0:T(8,128)}) async-done(((f32[16,1024]{1,0:T(8,128)}, f32[16,1024]{1,0:T(8,128)}), (f32[16,1024]{1,0:T(8,128)}, f32[16,1024]{1,0:T(8,128)})) %all-reduce.11.cloned.1.call-update) | async-done | bytes 131088 | tf_op jit(solution)/shard_map/psum | solution.py:41
  277.6 1.1 convolution_add_fusion
  278.6 10.1 %psum.93 = f32[16,256]{1,0:T(8,128)S(1)} all-reduce(f32[16,256]{1,0:T(8,128)S(1)} %convolution_add_fusion), channel_id=1, replica_groups=mesh['samp'=8,'var'=4] {'var'}, use_global_device_ids=true, to_apply=%region_13.0 | all-reduce | flops 4096 | bytes 32768 | tf_op jit(solution)/shard_map/psum | solution.py:33
  289.8 1.5 fusion.18
  291.4 1.5 fusion
  292.9 69.4 %all-reduce.9.cloned.1.call-done = (f32[16,1024]{1,0:T(8,128)}, f32[16,1024]{1,0:T(8,128)}) async-done(((f32[16,1024]{1,0:T(8,128)}, f32[16,1024]{1,0:T(8,128)}), (f32[16,1024]{1,0:T(8,128)}, f32[16,1024]{1,0:T(8,128)})) %all-reduce.9.cloned.1.call-update) | async-done | bytes 131088 | tf_op jit(solution)/shard_map/psum | solution.py:41
  362.2 1.5 add_divide_fusion
  (36 shorter events, 13.2 us)
Async XLA Ops:
  7.2 0.9 copy-start.1
  7.2 2.8 copy-start.3
  7.2 92.1 %all-reduce.15.cloned.1.call-start = ((), (), s32[]{:S(2)}) async-start(), calls=%async_computation.3 | async-start | bytes 262144 | tf_op jit(solution)/shard_map/psum | solution.py:41
  8.1 2.0 copy-start
  29.0 158.0 %all-reduce.13.cloned.1.call-start = ((), (), s32[]{:S(2)}) async-start(), calls=%async_computation.2 | async-start | bytes 262144 | tf_op jit(solution)/shard_map/psum | solution.py:41
  117.6 157.1 %all-reduce.11.cloned.1.call-start = ((), (), s32[]{:S(2)}) async-start(), calls=%async_computation.1 | async-start | bytes 262144 | tf_op jit(solution)/shard_map/psum | solution.py:41
  205.2 157.1 %all-reduce.9.cloned.1.call-start = ((), (), s32[]{:S(2)}) async-start(), calls=%async_computation | async-start | bytes 262144 | tf_op jit(solution)/shard_map/psum | solution.py:41
  288.8 2.6 copy-start.2
Sparse Core Ops, SparseCore 0:
  29.1 70.2 all-reduce.14
  117.7 69.2 all-reduce.12
  205.3 69.2 all-reduce.10
  293.0 69.2 all-reduce.8
where the time goes:
time: 371 us; the launch traced here: 370 us
  waiting for transfers between devices  278 us (75%)
  blocking collectives  43 us (12%)
  matrix products  29.6 us (8%)
  between operations  13.9 us (4%)
  other arithmetic  5.13 us (1%)
    psum x4, waiting for transfers between devices, shards(): sum_ref, sum_alt = lax.psum((term_ref, term_alt), 'samp')  278 us
    psum x4, blocking collectives, shards(): total = lax.psum(partial_value, 'var')  43 us
    dot_general x24, matrix products, contract(): lax.dot_general(left, right, (((left_dim,), (right_dim,)), ((), ())), pre...  29.6 us
  transfers between devices with their start and end apart: 4, of which 4 were waited for; matrix products, arithmetic and copies ran while one was open for 0% of the time, Pallas kernels for 0%

commit v1 on v0

--- a/solution.py
+++ b/solution.py
@@ -30,7 +30,8 @@
         partial_value = contract(frequency, ratio_ref, 1, 1) + contract(
             1.0 - frequency, ratio_alt, 1, 1
         )
-        total = lax.psum(partial_value, "var")
+        parts = lax.all_gather(partial_value, "var")
+        total = jnp.sum(parts, axis=0)
         weighted = fraction * total
         fraction = weighted / jnp.sum(weighted, axis=0, keepdims=True)
         expected = contract(fraction, frequency, 0, 0)

time: 371 us -> 351 us (0.946)
  blocking collectives: 43 us -> 21.9 us
    psum x4 -> x0, blocking collectives: 43 us -> none  [shards(): total = lax.psum(partial_value, 'var')]
    all_gather x0 -> x4, blocking collectives: none -> 21.9 us  [shards(): parts = lax.all_gather(partial_value, 'var')]
where the time goes in v1:
time: 351 us; the launch traced here: 350 us
  waiting for transfers between devices  279 us (79%)
  matrix products  29.6 us (8%)
  blocking collectives  21.9 us (6%)
  between operations  13.9 us (4%)
  other arithmetic  5.16 us (1%)
    psum x4, waiting for transfers between devices, shards(): sum_ref, sum_alt = lax.psum((term_ref, term_alt), 'samp')  279 us
    dot_general x24, matrix products, contract(): lax.dot_general(left, right, (((left_dim,), (right_dim,)), ((), ())), pre...  29.6 us
    all_gather x4, blocking collectives, shards(): parts = lax.all_gather(partial_value, 'var')  21.9 us
  transfers between devices with their start and end apart: 4, of which 4 were waited for; matrix products, arithmetic and copies ran while one was open for 0% of the time, Pallas kernels for 0%

profile of v1, /device:TPU:0, one launch (start us, length us, event | category | flops | bytes accessed | tf_op | source)
XLA Modules:
  0.0 350.4 jit_solution(1947079237208516178)
XLA Ops:
  8.1 1.9 fusion.36
  10.0 1.1 convolution_bitcast_fusion
  11.1 1.1 convolution_add_fusion.3
  12.2 6.2 %all-gather = f32[64,256]{1,0:T(8,128)S(1)} all-gather(f32[16,256]{1,0:T(8,128)S(1)} %convolution_add_fusion.3), channel_id=2, replica_groups=mesh['samp'=8,'var'=4] {'var'}, dimensions={0}, use_global_device_ids=true | all-gather | bytes 81920 | tf_op jit(solution)/shard_map/all_gather | solution.py:33
  19.5 1.5 fusion.15
  21.0 1.5 fusion.12
  22.5 71.8 %all-reduce.15.cloned.1.call-done = (f32[16,1024]{1,0:T(8,128)}, f32[16,1024]{1,0:T(8,128)}) async-done(((f32[16,1024]{1,0:T(8,128)}, f32[16,1024]{1,0:T(8,128)}), (f32[16,1024]{1,0:T(8,128)}, f32[16,1024]{1,0:T(8,128)})) %all-reduce.15.cloned.1.call-update) | async-done | bytes 131088 | tf_op jit(solution)/shard_map/psum | solution.py:42
  97.2 1.1 convolution_add_fusion.2
  98.3 5.2 %all-gather.1 = f32[64,256]{1,0:T(8,128)S(1)} all-gather(f32[16,256]{1,0:T(8,128)S(1)} %convolution_add_fusion.2), channel_id=3, replica_groups=mesh['samp'=8,'var'=4] {'var'}, dimensions={0}, use_global_device_ids=true | all-gather | bytes 81920 | tf_op jit(solution)/shard_map/all_gather | solution.py:33
  103.6 1.0 fusion.48
  104.6 1.5 fusion.16
  106.2 1.5 fusion.8
  107.9 69.1 %all-reduce.13.cloned.1.call-done = (f32[16,1024]{1,0:T(8,128)}, f32[16,1024]{1,0:T(8,128)}) async-done(((f32[16,1024]{1,0:T(8,128)}, f32[16,1024]{1,0:T(8,128)}), (f32[16,1024]{1,0:T(8,128)}, f32[16,1024]{1,0:T(8,128)})) %all-reduce.13.cloned.1.call-update) | async-done | bytes 131088 | tf_op jit(solution)/shard_map/psum | solution.py:42
  179.9 1.1 convolution_add_fusion.1
  181.0 5.2 %all-gather.2 = f32[64,256]{1,0:T(8,128)S(1)} all-gather(f32[16,256]{1,0:T(8,128)S(1)} %convolution_add_fusion.1), channel_id=4, replica_groups=mesh['samp'=8,'var'=4] {'var'}, dimensions={0}, use_global_device_ids=true | all-gather | bytes 81920 | tf_op jit(solution)/shard_map/all_gather | solution.py:33
  187.3 1.5 fusion.17
  188.9 1.5 fusion.4
  190.4 69.2 %all-reduce.11.cloned.1.call-done = (f32[16,1024]{1,0:T(8,128)}, f32[16,1024]{1,0:T(8,128)}) async-done(((f32[16,1024]{1,0:T(8,128)}, f32[16,1024]{1,0:T(8,128)}), (f32[16,1024]{1,0:T(8,128)}, f32[16,1024]{1,0:T(8,128)})) %all-reduce.11.cloned.1.call-update) | async-done | bytes 131088 | tf_op jit(solution)/shard_map/psum | solution.py:42
  262.6 1.1 convolution_add_fusion
  263.6 5.2 %all-gather.3 = f32[64,256]{1,0:T(8,128)S(1)} all-gather(f32[16,256]{1,0:T(8,128)S(1)} %convolution_add_fusion), channel_id=5, replica_groups=mesh['samp'=8,'var'=4] {'var'}, dimensions={0}, use_global_device_ids=true | all-gather | bytes 81920 | tf_op jit(solution)/shard_map/all_gather | solution.py:33
  270.0 1.5 fusion.18
  271.5 1.5 fusion
  273.0 69.3 %all-reduce.9.cloned.1.call-done = (f32[16,1024]{1,0:T(8,128)}, f32[16,1024]{1,0:T(8,128)}) async-done(((f32[16,1024]{1,0:T(8,128)}, f32[16,1024]{1,0:T(8,128)}), (f32[16,1024]{1,0:T(8,128)}, f32[16,1024]{1,0:T(8,128)})) %all-reduce.9.cloned.1.call-update) | async-done | bytes 131088 | tf_op jit(solution)/shard_map/psum | solution.py:42
  342.3 1.5 add_divide_fusion
  (40 shorter events, 13.3 us)
Async XLA Ops:
  7.2 0.9 copy-start.1
  7.2 2.8 copy-start.3
  7.2 87.1 %all-reduce.15.cloned.1.call-start = ((), (), s32[]{:S(2)}) async-start(), calls=%async_computation.3 | async-start | bytes 262144 | tf_op jit(solution)/shard_map/psum | solution.py:42
  8.1 2.0 copy-start
  22.5 154.5 %all-reduce.13.cloned.1.call-start = ((), (), s32[]{:S(2)}) async-start(), calls=%async_computation.2 | async-start | bytes 262144 | tf_op jit(solution)/shard_map/psum | solution.py:42
  107.7 152.0 %all-reduce.11.cloned.1.call-start = ((), (), s32[]{:S(2)}) async-start(), calls=%async_computation.1 | async-start | bytes 262144 | tf_op jit(solution)/shard_map/psum | solution.py:42
  190.3 152.0 %all-reduce.9.cloned.1.call-start = ((), (), s32[]{:S(2)}) async-start(), calls=%async_computation | async-start | bytes 262144 | tf_op jit(solution)/shard_map/psum | solution.py:42
  268.9 2.6 copy-start.2
Sparse Core Ops, SparseCore 0:
  22.6 71.6 all-reduce.14
  107.8 69.1 all-reduce.12
  190.5 69.1 all-reduce.10
  273.1 69.1 all-reduce.8
